TPU v7x, 32 devices: a whole 2x2x4 slice. The times are simulated.
32 devices in a mesh: groups: 2 (over y), space: 16 (over z, x, core).
Axes of the slice: x: 2, y: 2, z: 4, core: 2. Of those that a mesh axis runs over, the one named last changes fastest.
Arguments:
- coarse_input: bfloat16 [256, 16, 256], P('groups', 'space'), parts along dimension 0, may hold values from -6 to 6
- skip: bfloat16 [128, 32, 1024], P('groups', None, 'space'), parts along dimension 0, may hold values from -6 to 6
- cotangent: bfloat16 [128, 32, 1024], P('groups', 'space'), parts along dimension 0, may hold values from -6 to 6
- w_up: bfloat16 [8, 64, 128], replicated, may hold values from -0.5 to 0.5
- w_conv: bfloat16 [27, 64, 128], replicated, may hold values from -0.109375 to 0.109375
Outputs:
- activation: bfloat16 [128, 32, 1024], P('groups', 'space'), parts along dimension 0
- grad_input: bfloat16 [256, 16, 256], P('groups', 'space'), parts along dimension 0
- grad_skip: bfloat16 [128, 32, 1024], P('groups', None, 'space'), parts along dimension 0
- grad_w_up: float32 [16, 64, 128], P('groups'), parts along dimension 0
- grad_w_conv: float32 [54, 64, 128], P('groups'), parts along dimension 0
There are 2 independent parts, one for each index of `groups`. A program takes and returns all parts, laid end to end along the dimension named above; an argument that names none is the same for every part. Nothing has to cross between parts.
All inputs are finite; a program needn't handle non-finite values.
Results may differ from a plain program's by a relative error of at most 0.012.
Values may be sent and summed in bfloat16 or wider, within the bound.
A program may use at most 64 MiB of HBM per device.

v0:
```python
import math

import jax
import jax.numpy as jnp
from jax import lax
from jax.sharding import PartitionSpec as P

W = 128


def padded_2(value, sides, width):
    for axis, dim in sides:
        peers, length = (lax.axis_size(axis), value.shape[dim])
        up = [(i, (i + 1) % peers) for i in range(peers - 1)]
        down = [(j, i) for i, j in up]
        last = lax.slice_in_dim(value, length - width, length, axis=dim)
        leading = lax.slice_in_dim(value, 0, width, axis=dim)
        before = lax.ppermute(last, axis, up)
        after = lax.ppermute(leading, axis, down)
        value = jnp.concatenate([before, value, after], axis=dim)
    return value


def upsample(coarse, w_up, height, width):
    channels = coarse.shape[0]
    planes = coarse.shape[1]
    outputs = w_up.shape[1]
    terms = jnp.dot(
        w_up.reshape(8 * outputs, channels),
        coarse.reshape(channels, -1),
        preferred_element_type=jnp.float32,
    )
    terms = terms.reshape(2, 2, 2, outputs, planes, height // 2, width // 2)
    terms = terms.transpose(3, 4, 0, 5, 1, 6, 2)
    return terms.reshape(outputs, 2 * planes, height, width).astype(jnp.bfloat16)


def pad_sides(volume):
    return jnp.pad(volume, ((0, 0), (0, 0), (1, 1), (1, 1)))


def conv_forward(padded, w_conv, planes, height, width):
    channels = padded.shape[0]
    total = jnp.zeros((w_conv.shape[1], planes * height * width), jnp.float32)
    for depth_tap in range(3):
        for row_tap in range(3):
            for col_tap in range(3):
                window = padded[
                    :,
                    depth_tap : depth_tap + planes,
                    row_tap : row_tap + height,
                    col_tap : col_tap + width,
                ].reshape(channels, -1)
                total = total + jnp.dot(
                    w_conv[9 * depth_tap + 3 * row_tap + col_tap],
                    window,
                    preferred_element_type=jnp.float32,
                )
    return total


def conv_input_grad(padded, w_conv, planes, height, width):
    channels = padded.shape[0]
    total = jnp.zeros((w_conv.shape[2], planes * height * width), jnp.float32)
    for depth_tap in range(3):
        for row_tap in range(3):
            for col_tap in range(3):
                window = padded[
                    :,
                    2 - depth_tap : 2 - depth_tap + planes,
                    2 - row_tap : 2 - row_tap + height,
                    2 - col_tap : 2 - col_tap + width,
                ].reshape(channels, -1)
                total = total + lax.dot_general(
                    w_conv[9 * depth_tap + 3 * row_tap + col_tap],
                    window,
                    (((0,), (0,)), ((), ())),
                    preferred_element_type=jnp.float32,
                )
    return total


def conv_weight_grad(padded, grad_flat, planes, height, width):
    channels = padded.shape[0]
    results = []
    for depth_tap in range(3):
        for row_tap in range(3):
            for col_tap in range(3):
                window = padded[
                    :,
                    depth_tap : depth_tap + planes,
                    row_tap : row_tap + height,
                    col_tap : col_tap + width,
                ].reshape(channels, -1)
                results.append(
                    lax.dot_general(
                        grad_flat,
                        window,
                        (((1,), (1,)), ((), ())),
                        preferred_element_type=jnp.float32,
                    )
                )
    return jnp.stack(results, 0)


def local(coarse_input, skip, cotangent, w_up, w_conv):
    devices = lax.axis_size("space")
    channels_in = coarse_input.shape[0]
    coarse_planes = coarse_input.shape[1]
    up_channels = w_up.shape[1]
    skip_channels = skip.shape[0]
    out_channels = cotangent.shape[0]
    planes = cotangent.shape[1]
    cells = cotangent.shape[2]
    width = W
    height = cells // width
    joined_channels = up_channels + skip_channels
    skip_local = lax.all_to_all(skip, "space", split_axis=1, concat_axis=2, tiled=True)
    upsampled = upsample(coarse_input, w_up, height, width)
    joined = jnp.concatenate([upsampled.reshape(up_channels, planes, cells), skip_local], 0)
    joined_ext = padded_2(joined, (("space", 1),), 1)
    joined_pad = pad_sides(joined_ext.reshape(joined_channels, planes + 2, height, width))
    pre = conv_forward(joined_pad, w_conv, planes, height, width)
    gate = jax.nn.sigmoid(pre)
    activation = (pre * gate).astype(jnp.bfloat16).reshape(out_channels, planes, cells)
    grad_pre = (
        cotangent.reshape(out_channels, -1).astype(jnp.float32) * gate * (1.0 + pre * (1.0 - gate))
    ).astype(jnp.bfloat16)
    grad_ext = padded_2(grad_pre.reshape(out_channels, planes, cells), (("space", 1),), 1)
    grad_pad = pad_sides(grad_ext.reshape(out_channels, planes + 2, height, width))
    grad_joined = conv_input_grad(grad_pad, w_conv, planes, height, width)
    grad_up = grad_joined[:up_channels].astype(jnp.bfloat16)
    skip_part = grad_joined[up_channels:].astype(jnp.bfloat16).reshape(skip_channels, planes, cells)
    grad_skip = lax.all_to_all(skip_part, "space", split_axis=2, concat_axis=1, tiled=True)
    arranged = (
        grad_up.reshape(up_channels, coarse_planes, 2, height // 2, 2, width // 2, 2)
        .transpose(2, 4, 6, 0, 1, 3, 5)
        .reshape(8 * up_channels, -1)
    )
    flat_up = w_up.reshape(8 * up_channels, channels_in)
    grad_input = lax.dot_general(
        flat_up, arranged, (((0,), (0,)), ((), ())), preferred_element_type=jnp.float32
    )
    grad_input = grad_input.astype(jnp.bfloat16).reshape(channels_in, coarse_planes, -1)
    local_up = lax.dot_general(
        arranged,
        coarse_input.reshape(channels_in, -1),
        (((1,), (1,)), ((), ())),
        preferred_element_type=jnp.float32,
    )
    local_up = local_up.reshape(8, up_channels, channels_in)
    local_conv = conv_weight_grad(joined_pad, grad_pre, planes, height, width)
    scale = 1.0 / math.sqrt(devices * planes * cells)
    summed_up, summed_conv = lax.psum((local_up * scale, local_conv * scale), "space")
    return (activation, grad_input, grad_skip, summed_up, summed_conv)


def solution(mesh):
    in_specs = (
        P("groups", "space", None),
        P("groups", None, "space"),
        P("groups", "space", None),
        P(),
        P(),
    )
    out_specs = (
        P("groups", "space", None),
        P("groups", "space", None),
        P("groups", None, "space"),
        P("groups", None, None),
        P("groups", None, None),
    )
    return jax.shard_map(local, mesh=mesh, in_specs=in_specs, out_specs=out_specs, check_vma=False)
```

profile of v0, /device:TPU:0, one launch (start us, length us, event | category | flops | bytes accessed | tf_op | source)
XLA Modules:
  0.0 211.5 jit_solution(14226043892768024418)
XLA Ops:
  7.2 1.3 copy.209
  8.5 1.1 reshape.319
  9.6 7.4 %all-to-all-start = ((bf16[16,2,4096]{2,1,0:T(2,128)(2,1)}), bf16[16,2,4096]{2,1,0:T(2,128)(2,1)S(1)}, u32[]{:S(2)}, u32[]{:S(2)}) async-start(bf16[16,2,4096]{2,1,0:T(2,128)(2,1)} %reshape.319), calls=%async_computation | async-start | bytes 524288 | tf_op jit(solution)/shard_map/all_to_all | solution.py:118
  17.9 9.1 %all-to-all-done = bf16[16,2,4096]{2,1,0:T(2,128)(2,1)S(1)} async-done(((bf16[16,2,4096]{2,1,0:T(2,128)(2,1)}), bf16[16,2,4096]{2,1,0:T(2,128)(2,1)S(1)}, u32[]{:S(2)}, u32[]{:S(2)}) %all-to-all-start) | async-done | bytes 262176 | tf_op jit(solution)/shard_map/all_to_all | solution.py:118
  27.9 1.8 collective-permute-start
  29.7 1.3 collective-permute-start.1
  31.1 2.0 collective-permute-done.1
  33.5 3.6 %pad_slice_fusion = (bf16[128,2,8,128]{0,3,2,1:T(8,128)(2,1)S(1)}, bf16[128,2,8,128]{0,3,2,1:T(8,128)(2,1)S(1)}, bf16[128,2,8,128]{0,3,2,1:T(8,128)(2,1)S(1)}, b...) fusion(bf16[128,4,8,128]{0,3,2,1:T(8,128)(2,1)S(1)} %bitcast.654), kind=kLoop, calls=%fused_computation.87 | loop fusion | bytes 11010048 | tf_op jit(solution)/shard_map/slice | solution.py:48
  46.7 1.1 multiply_convert_fusion
  48.6 0.9 reshape.283
  49.5 2.0 fusion.56
  51.5 1.9 fusion.55
  53.5 1.9 fusion.54
  55.4 0.8 fusion.53
  56.3 0.8 fusion.52
  57.1 0.8 fusion.51
  58.0 0.8 fusion.50
  58.8 0.8 fusion.49
  59.6 0.8 fusion.48
  60.5 0.8 fusion.47
  61.3 0.8 fusion.46
  62.2 0.8 fusion.45
  63.0 0.8 fusion.44
  63.9 0.8 fusion.43
  64.7 0.8 fusion.42
  65.6 0.8 fusion.41
  66.4 0.8 fusion.40
  67.3 0.8 fusion.39
  68.1 0.8 fusion.38
  69.0 0.8 fusion.37
  70.7 0.8 fusion.35
  71.5 0.8 fusion.34
  72.4 0.8 fusion.33
  73.2 0.8 fusion.32
  75.3 6.4 %collective-permute-start.2 = (bf16[64,1,1024]{2,0,1:T(8,128)(2,1)S(1)}, bf16[64,1,1024]{2,0,1:T(8,128)(2,1)S(1)}, u32[]{:S(2)}, u32[]{:S(2)}) collective-permute-start(bf16[64,1,1024]{2,0,1:T(8,128)(2,1)S(1)} %copy.72), channel_id=1, source_target_pairs={{0,1},{1,2},{2,3},{3,4},{4,5},{5,6},{6,7},{7,8},{8,9},{9,10},{10,1... | collective-permute-start | bytes 393224 | tf_op jit(solution)/shard_map/ppermute | solution.py:18
  81.7 1.3 collective-permute-start.3
  83.1 1.0 broadcast_multiply_fusion
  85.1 1.9 select_maximum_fusion
  87.5 1.5 fusion.222
  99.6 0.9 convolution_multiply_fusion
  101.2 1.1 reshape.321
  102.3 8.6 %all-to-all-start.1 = ((bf16[16,2,4096]{2,1,0:T(2,128)(2,1)}), bf16[16,2,4096]{2,1,0:T(2,128)(2,1)S(1)}, u32[]{:S(2)}, u32[]{:S(2)}) async-start(bf16[16,2,4096]{2,1,0:T(2,128)(2,1)} %reshape.321), calls=%async_computation.1 | async-start | bytes 524288 | tf_op jit(solution)/shard_map/all_to_all | solution.py:134
  111.0 0.9 reshape.282
  113.2 9.6 %all-to-all-done.1 = bf16[16,2,4096]{2,1,0:T(2,128)(2,1)S(1)} async-done(((bf16[16,2,4096]{2,1,0:T(2,128)(2,1)}), bf16[16,2,4096]{2,1,0:T(2,128)(2,1)S(1)}, u32[]{:S(2)}, u32[]{:S(2)}) %all-to-all-start.1) | async-done | bytes 262176 | tf_op jit(solution)/shard_map/all_to_all | solution.py:134
  123.2 2.2 %copy.62 = bf16[64,16,2,64]{3,2,1,0:T(2,128)(2,1)} copy(bf16[64,16,2,64]{0,2,3,1:T(2,128)(2,1)S(1)} %bitcast.717) | data formatting | bytes 524288 | tf_op jit(solution)/shard_map/all_to_all | solution.py:134
  125.4 75.4 %all-reduce.5.cloned.1.call-done = (f32[8,64,128]{2,1,0:T(8,128)}, f32[27,64,128]{2,1,0:T(8,128)}) async-done(((f32[8,64,128]{2,1,0:T(8,128)}, f32[27,64,128]{2,1,0:T(8,128)}), (f32[8,64,128]{2,1,0:T(8,128)}, f32[27,64,128]{2,1,0:T(8,128)})) %all-reduce.5.cloned.1.call-update) | async-done | bytes 1146896 | tf_op jit(solution)/shard_map/psum | solution.py:154
  200.9 1.7 copy.238
  202.5 2.2 %copy.239 = f32[27,64,128]{2,1,0:T(8,128)} copy(f32[27,64,128]{2,1,0:T(8,128)} %get-tuple-element.92) | data formatting | bytes 1769472
  (180 shorter events, 28.5 us)
Async XLA Ops:
  7.2 10.0 %copy-start = (bf16[8,64,128]{2,1,0:T(8,128)(2,1)S(1)}, bf16[8,64,128]{2,1,0:T(8,128)(2,1)}, u32[]{:S(2)}) copy-start(bf16[8,64,128]{2,1,0:T(8,128)(2,1)} %param.8) | copy-start | bytes 393220
  7.2 9.8 %copy-start.43 = (bf16[128,1,256]{2,0,1:T(8,128)(2,1)S(1)}, bf16[128,1,256]{2,0,1:T(8,128)(2,1)}, u32[]{:S(2)}) copy-start(bf16[128,1,256]{2,0,1:T(8,128)(2,1)} %param.5) | copy-start | bytes 196612
  9.6 17.4 %all-to-all-start = ((bf16[16,2,4096]{2,1,0:T(2,128)(2,1)}), bf16[16,2,4096]{2,1,0:T(2,128)(2,1)S(1)}, u32[]{:S(2)}, u32[]{:S(2)}) async-start(bf16[16,2,4096]{2,1,0:T(2,128)(2,1)} %reshape.319), calls=%async_computation | async-start | bytes 524288 | tf_op jit(solution)/shard_map/all_to_all | solution.py:118
  17.0 183.9 %all-reduce.5.cloned.1.call-start = ((), (), s32[]{:S(2)}) async-start(), calls=%async_computation.2 | async-start | bytes 2293760 | tf_op jit(solution)/shard_map/psum | solution.py:154
  17.5 13.6 %copy-start.42 = (bf16[64,2,1024]{2,1,0:T(2,128)(2,1)S(1)}, bf16[64,2,1024]{2,1,0:T(2,128)(2,1)}, u32[]{:S(2)}) copy-start(bf16[64,2,1024]{2,1,0:T(2,128)(2,1)} %param.7) | copy-start | bytes 786436
  27.9 3.2 %collective-permute-start = (bf16[128,1,1024]{0,2,1:T(8,128)(2,1)S(1)}, bf16[128,1,1024]{0,2,1:T(8,128)(2,1)S(1)}, u32[]{:S(2)}, u32[]{:S(2)}) collective-permute-start(bf16[128,1,1024]{0,2,1:T(8,128)(2,1)S(1)} %get-tuple-element.78), channel_id=1, source_target_pairs={{0,1},{1,2},{2,3},{3,4},{4,5},{5,6},{6,7},{7,8},{8,9},{9,10},{10,1... | collective-permute-start | bytes 786440 | tf_op jit(solution)/shard_map/ppermute | solution.py:18
  29.7 3.4 %collective-permute-start.1 = (bf16[128,1,1024]{0,2,1:T(8,128)(2,1)S(1)}, bf16[128,1,1024]{0,2,1:T(8,128)(2,1)S(1)}, u32[]{:S(2)}, u32[]{:S(2)}) collective-permute-start(bf16[128,1,1024]{0,2,1:T(8,128)(2,1)S(1)} %get-tuple-element.79), channel_id=1, source_target_pairs={{1,0},{2,1},{3,2},{4,3},{5,4},{6,5},{7,6},{8,7},{9,8},{10,9},{11,1... | collective-permute-start | bytes 786440 | tf_op jit(solution)/shard_map/ppermute | solution.py:19
  37.1 2.4 %copy-start.33 = (bf16[128,2,8,128]{0,3,2,1:T(8,128)(2,1)}, bf16[128,2,8,128]{0,3,2,1:T(8,128)(2,1)S(1)}, u32[]{:S(2)}) copy-start(bf16[128,2,8,128]{0,3,2,1:T(8,128)(2,1)S(1)} %get-tuple-element.54) | copy-start | bytes 1572868
  37.1 2.7 %copy-start.35 = (bf16[128,2,8,128]{0,3,2,1:T(8,128)(2,1)}, bf16[128,2,8,128]{0,3,2,1:T(8,128)(2,1)S(1)}, u32[]{:S(2)}) copy-start(bf16[128,2,8,128]{0,3,2,1:T(8,128)(2,1)S(1)} %get-tuple-element.52) | copy-start | bytes 1572868
  37.1 3.0 %copy-start.31 = (bf16[128,2,8,128]{0,3,2,1:T(8,128)(2,1)}, bf16[128,2,8,128]{0,3,2,1:T(8,128)(2,1)S(1)}, u32[]{:S(2)}) copy-start(bf16[128,2,8,128]{0,3,2,1:T(8,128)(2,1)S(1)} %get-tuple-element.55) | copy-start | bytes 1572868
  37.1 3.3 %copy-start.29 = (bf16[128,2,8,128]{0,3,2,1:T(8,128)(2,1)}, bf16[128,2,8,128]{0,3,2,1:T(8,128)(2,1)S(1)}, u32[]{:S(2)}) copy-start(bf16[128,2,8,128]{0,3,2,1:T(8,128)(2,1)S(1)} %get-tuple-element.56) | copy-start | bytes 1572868
  37.1 3.6 %copy-start.27 = (bf16[128,2,8,128]{0,3,2,1:T(8,128)(2,1)}, bf16[128,2,8,128]{0,3,2,1:T(8,128)(2,1)S(1)}, u32[]{:S(2)}) copy-start(bf16[128,2,8,128]{0,3,2,1:T(8,128)(2,1)S(1)} %get-tuple-element.57) | copy-start | bytes 1572868
  37.1 3.9 %copy-start.25 = (bf16[128,2,8,128]{0,3,2,1:T(8,128)(2,1)}, bf16[128,2,8,128]{0,3,2,1:T(8,128)(2,1)S(1)}, u32[]{:S(2)}) copy-start(bf16[128,2,8,128]{0,3,2,1:T(8,128)(2,1)S(1)} %get-tuple-element.58) | copy-start | bytes 1572868
  37.1 4.3 %copy-start.23 = (bf16[128,2,8,128]{0,3,2,1:T(8,128)(2,1)}, bf16[128,2,8,128]{0,3,2,1:T(8,128)(2,1)S(1)}, u32[]{:S(2)}) copy-start(bf16[128,2,8,128]{0,3,2,1:T(8,128)(2,1)S(1)} %get-tuple-element.59) | copy-start | bytes 1572868
  37.1 4.6 %copy-start.21 = (bf16[128,2,8,128]{0,3,2,1:T(8,128)(2,1)}, bf16[128,2,8,128]{0,3,2,1:T(8,128)(2,1)S(1)}, u32[]{:S(2)}) copy-start(bf16[128,2,8,128]{0,3,2,1:T(8,128)(2,1)S(1)} %get-tuple-element.60) | copy-start | bytes 1572868
  37.2 4.9 %copy-start.19 = (bf16[128,2,8,128]{0,3,2,1:T(8,128)(2,1)}, bf16[128,2,8,128]{0,3,2,1:T(8,128)(2,1)S(1)}, u32[]{:S(2)}) copy-start(bf16[128,2,8,128]{0,3,2,1:T(8,128)(2,1)S(1)} %get-tuple-element.61) | copy-start | bytes 1572868
  37.2 5.2 %copy-start.17 = (bf16[128,2,8,128]{0,3,2,1:T(8,128)(2,1)}, bf16[128,2,8,128]{0,3,2,1:T(8,128)(2,1)S(1)}, u32[]{:S(2)}) copy-start(bf16[128,2,8,128]{0,3,2,1:T(8,128)(2,1)S(1)} %get-tuple-element.62) | copy-start | bytes 1572868
  37.2 5.8 %copy-start.15 = (bf16[128,2,8,128]{0,3,2,1:T(8,128)(2,1)}, bf16[128,2,8,128]{0,3,2,1:T(8,128)(2,1)S(1)}, u32[]{:S(2)}) copy-start(bf16[128,2,8,128]{0,3,2,1:T(8,128)(2,1)S(1)} %get-tuple-element.63) | copy-start | bytes 1572868
  37.2 6.1 %copy-start.13 = (bf16[128,2,8,128]{0,3,2,1:T(8,128)(2,1)}, bf16[128,2,8,128]{0,3,2,1:T(8,128)(2,1)S(1)}, u32[]{:S(2)}) copy-start(bf16[128,2,8,128]{0,3,2,1:T(8,128)(2,1)S(1)} %get-tuple-element.64) | copy-start | bytes 1572868
  37.2 6.4 %copy-start.11 = (bf16[128,2,8,128]{0,3,2,1:T(8,128)(2,1)}, bf16[128,2,8,128]{0,3,2,1:T(8,128)(2,1)S(1)}, u32[]{:S(2)}) copy-start(bf16[128,2,8,128]{0,3,2,1:T(8,128)(2,1)S(1)} %get-tuple-element.65) | copy-start | bytes 1572868
  37.2 6.7 %copy-start.9 = (bf16[128,2,8,128]{0,3,2,1:T(8,128)(2,1)}, bf16[128,2,8,128]{0,3,2,1:T(8,128)(2,1)S(1)}, u32[]{:S(2)}) copy-start(bf16[128,2,8,128]{0,3,2,1:T(8,128)(2,1)S(1)} %get-tuple-element.66) | copy-start | bytes 1572868
  37.2 7.0 %copy-start.7 = (bf16[128,2,8,128]{0,3,2,1:T(8,128)(2,1)}, bf16[128,2,8,128]{0,3,2,1:T(8,128)(2,1)S(1)}, u32[]{:S(2)}) copy-start(bf16[128,2,8,128]{0,3,2,1:T(8,128)(2,1)S(1)} %get-tuple-element.67) | copy-start | bytes 1572868
  37.2 7.3 %copy-start.5 = (bf16[128,2,8,128]{0,3,2,1:T(8,128)(2,1)}, bf16[128,2,8,128]{0,3,2,1:T(8,128)(2,1)S(1)}, u32[]{:S(2)}) copy-start(bf16[128,2,8,128]{0,3,2,1:T(8,128)(2,1)S(1)} %get-tuple-element.68) | copy-start | bytes 1572868
  37.2 7.6 %copy-start.3 = (bf16[128,2,8,128]{0,3,2,1:T(8,128)(2,1)}, bf16[128,2,8,128]{0,3,2,1:T(8,128)(2,1)S(1)}, u32[]{:S(2)}) copy-start(bf16[128,2,8,128]{0,3,2,1:T(8,128)(2,1)S(1)} %get-tuple-element.69) | copy-start | bytes 1572868
  37.2 9.4 %copy-start.37 = (bf16[128,2,8,128]{0,3,2,1:T(8,128)(2,1)}, bf16[128,2,8,128]{0,3,2,1:T(8,128)(2,1)S(1)}, u32[]{:S(2)}) copy-start(bf16[128,2,8,128]{0,3,2,1:T(8,128)(2,1)S(1)} %get-tuple-element.51) | copy-start | bytes 1572868
  49.5 5.9 %copy-start.2 = (bf16[128,2,8,128]{0,3,2,1:T(8,128)(2,1)S(1)}, bf16[128,2,8,128]{0,3,2,1:T(8,128)(2,1)}, u32[]{:S(2)}) copy-start(bf16[128,2,8,128]{0,3,2,1:T(8,128)(2,1)} %copy-done.1) | copy-start | bytes 1572868
  49.5 6.7 %copy-start.32 = (bf16[128,2,8,128]{0,3,2,1:T(8,128)(2,1)S(1)}, bf16[128,2,8,128]{0,3,2,1:T(8,128)(2,1)}, u32[]{:S(2)}) copy-start(bf16[128,2,8,128]{0,3,2,1:T(8,128)(2,1)} %copy-done.31) | copy-start | bytes 1572868
  49.5 7.6 %copy-start.30 = (bf16[128,2,8,128]{0,3,2,1:T(8,128)(2,1)S(1)}, bf16[128,2,8,128]{0,3,2,1:T(8,128)(2,1)}, u32[]{:S(2)}) copy-start(bf16[128,2,8,128]{0,3,2,1:T(8,128)(2,1)} %copy-done.29) | copy-start | bytes 1572868
  51.5 6.4 %copy-start.28 = (bf16[128,2,8,128]{0,3,2,1:T(8,128)(2,1)S(1)}, bf16[128,2,8,128]{0,3,2,1:T(8,128)(2,1)}, u32[]{:S(2)}) copy-start(bf16[128,2,8,128]{0,3,2,1:T(8,128)(2,1)} %copy-done.27) | copy-start | bytes 1572868
  53.5 5.3 %copy-start.26 = (bf16[128,2,8,128]{0,3,2,1:T(8,128)(2,1)S(1)}, bf16[128,2,8,128]{0,3,2,1:T(8,128)(2,1)}, u32[]{:S(2)}) copy-start(bf16[128,2,8,128]{0,3,2,1:T(8,128)(2,1)} %copy-done.25) | copy-start | bytes 1572868
  55.4 4.2 %copy-start.24 = (bf16[128,2,8,128]{0,3,2,1:T(8,128)(2,1)S(1)}, bf16[128,2,8,128]{0,3,2,1:T(8,128)(2,1)}, u32[]{:S(2)}) copy-start(bf16[128,2,8,128]{0,3,2,1:T(8,128)(2,1)} %copy-done.23) | copy-start | bytes 1572868
  56.2 4.2 %copy-start.22 = (bf16[128,2,8,128]{0,3,2,1:T(8,128)(2,1)S(1)}, bf16[128,2,8,128]{0,3,2,1:T(8,128)(2,1)}, u32[]{:S(2)}) copy-start(bf16[128,2,8,128]{0,3,2,1:T(8,128)(2,1)} %copy-done.21) | copy-start | bytes 1572868
  57.1 4.2 %copy-start.20 = (bf16[128,2,8,128]{0,3,2,1:T(8,128)(2,1)S(1)}, bf16[128,2,8,128]{0,3,2,1:T(8,128)(2,1)}, u32[]{:S(2)}) copy-start(bf16[128,2,8,128]{0,3,2,1:T(8,128)(2,1)} %copy-done.19) | copy-start | bytes 1572868
  58.0 4.2 %copy-start.18 = (bf16[128,2,8,128]{0,3,2,1:T(8,128)(2,1)S(1)}, bf16[128,2,8,128]{0,3,2,1:T(8,128)(2,1)}, u32[]{:S(2)}) copy-start(bf16[128,2,8,128]{0,3,2,1:T(8,128)(2,1)} %copy-done.17) | copy-start | bytes 1572868
  59.6 4.2 %copy-start.16 = (bf16[128,2,8,128]{0,3,2,1:T(8,128)(2,1)S(1)}, bf16[128,2,8,128]{0,3,2,1:T(8,128)(2,1)}, u32[]{:S(2)}) copy-start(bf16[128,2,8,128]{0,3,2,1:T(8,128)(2,1)} %copy-done.15) | copy-start | bytes 1572868
  60.5 4.2 %copy-start.14 = (bf16[128,2,8,128]{0,3,2,1:T(8,128)(2,1)S(1)}, bf16[128,2,8,128]{0,3,2,1:T(8,128)(2,1)}, u32[]{:S(2)}) copy-start(bf16[128,2,8,128]{0,3,2,1:T(8,128)(2,1)} %copy-done.13) | copy-start | bytes 1572868
  61.3 4.2 %copy-start.12 = (bf16[128,2,8,128]{0,3,2,1:T(8,128)(2,1)S(1)}, bf16[128,2,8,128]{0,3,2,1:T(8,128)(2,1)}, u32[]{:S(2)}) copy-start(bf16[128,2,8,128]{0,3,2,1:T(8,128)(2,1)} %copy-done.11) | copy-start | bytes 1572868
  62.2 4.2 %copy-start.10 = (bf16[128,2,8,128]{0,3,2,1:T(8,128)(2,1)S(1)}, bf16[128,2,8,128]{0,3,2,1:T(8,128)(2,1)}, u32[]{:S(2)}) copy-start(bf16[128,2,8,128]{0,3,2,1:T(8,128)(2,1)} %copy-done.9) | copy-start | bytes 1572868
  63.0 4.2 %copy-start.8 = (bf16[128,2,8,128]{0,3,2,1:T(8,128)(2,1)S(1)}, bf16[128,2,8,128]{0,3,2,1:T(8,128)(2,1)}, u32[]{:S(2)}) copy-start(bf16[128,2,8,128]{0,3,2,1:T(8,128)(2,1)} %copy-done.7) | copy-start | bytes 1572868
  63.9 4.2 %copy-start.6 = (bf16[128,2,8,128]{0,3,2,1:T(8,128)(2,1)S(1)}, bf16[128,2,8,128]{0,3,2,1:T(8,128)(2,1)}, u32[]{:S(2)}) copy-start(bf16[128,2,8,128]{0,3,2,1:T(8,128)(2,1)} %copy-done.5) | copy-start | bytes 1572868
  64.7 4.2 %copy-start.4 = (bf16[128,2,8,128]{0,3,2,1:T(8,128)(2,1)S(1)}, bf16[128,2,8,128]{0,3,2,1:T(8,128)(2,1)}, u32[]{:S(2)}) copy-start(bf16[128,2,8,128]{0,3,2,1:T(8,128)(2,1)} %copy-done.3) | copy-start | bytes 1572868
  69.8 4.2 %copy-start.38 = (bf16[128,2,8,128]{0,3,2,1:T(8,128)(2,1)S(1)}, bf16[128,2,8,128]{0,3,2,1:T(8,128)(2,1)}, u32[]{:S(2)}) copy-start(bf16[128,2,8,128]{0,3,2,1:T(8,128)(2,1)} %copy-done.37) | copy-start | bytes 1572868
  70.7 4.2 %copy-start.36 = (bf16[64,2,1024]{2,1,0:T(2,128)(2,1)S(1)}, bf16[64,2,1024]{2,1,0:T(2,128)(2,1)}, u32[]{:S(2)}) copy-start(bf16[64,2,1024]{2,1,0:T(2,128)(2,1)} %reshape.283) | copy-start | bytes 786436
  74.9 8.2 %copy-start.41 = (f32[27,64,128]{2,1,0:T(8,128)S(1)}, f32[27,64,128]{2,1,0:T(8,128)}, u32[]{:S(2)}) copy-start(f32[27,64,128]{2,1,0:T(8,128)} %fusion.31) | copy-start | bytes 2654212
  75.3 8.8 %collective-permute-start.2 = (bf16[64,1,1024]{2,0,1:T(8,128)(2,1)S(1)}, bf16[64,1,1024]{2,0,1:T(8,128)(2,1)S(1)}, u32[]{:S(2)}, u32[]{:S(2)}) collective-permute-start(bf16[64,1,1024]{2,0,1:T(8,128)(2,1)S(1)} %copy.72), channel_id=1, source_target_pairs={{0,1},{1,2},{2,3},{3,4},{4,5},{5,6},{6,7},{7,8},{8,9},{9,10},{10,1... | collective-permute-start | bytes 393224 | tf_op jit(solution)/shard_map/ppermute | solution.py:18
  81.7 3.2 %collective-permute-start.3 = (bf16[64,1,1024]{2,0,1:T(8,128)(2,1)S(1)}, bf16[64,1,1024]{2,0,1:T(8,128)(2,1)S(1)}, u32[]{:S(2)}, u32[]{:S(2)}) collective-permute-start(bf16[64,1,1024]{2,0,1:T(8,128)(2,1)S(1)} %copy.73), channel_id=1, source_target_pairs={{1,0},{2,1},{3,2},{4,3},{5,4},{6,5},{7,6},{8,7},{9,8},{10,9},{11,1... | collective-permute-start | bytes 393224 | tf_op jit(solution)/shard_map/ppermute | solution.py:19
  99.6 11.4 %copy-start.45 = (bf16[64,2048]{1,0:T(8,128)(2,1)S(1)}, bf16[64,2048]{1,0:T(8,128)(2,1)}, u32[]{:S(2)}) copy-start(bf16[64,2048]{1,0:T(8,128)(2,1)} %get-tuple-element.83) | copy-start | bytes 786436
  102.3 20.5 %all-to-all-start.1 = ((bf16[16,2,4096]{2,1,0:T(2,128)(2,1)}), bf16[16,2,4096]{2,1,0:T(2,128)(2,1)S(1)}, u32[]{:S(2)}, u32[]{:S(2)}) async-start(bf16[16,2,4096]{2,1,0:T(2,128)(2,1)} %reshape.321), calls=%async_computation.1 | async-start | bytes 524288 | tf_op jit(solution)/shard_map/all_to_all | solution.py:134
  (5 other events, 7.9 us)
Sparse Core Ops, SparseCore 0:
  100.7 100.1 all-reduce.4
where the time goes:
time: 212 us
  waiting for transfers between devices  97.1 us (46%)
  matrix products  45.7 us (22%)
  starting transfers between devices  26.8 us (13%)
  local copies, waits for them, and re-layouts  23.3 us (11%)
  between operations  15.1 us (7%)
  other arithmetic  3.59 us (2%)
    psum x1, waiting for transfers between devices, local(): lax.psum((local_up * scale, local_conv * scale), 'space')  75.4 us
    dot_general x27, matrix products, conv_weight_grad(): lax.dot_general(grad_flat, window, (((1,), (1,)), ((), ())), preferred_el...  26.1 us
    unnamed x107, local copies, waits for them, and re-layouts  9.8 us
    all_to_all x1, waiting for transfers between devices, local(): lax.all_to_all(skip_part, 'space', split_axis=2, concat_axis=1, tiled=True)  9.63 us
    dot_general x27, matrix products, conv_input_grad(): lax.dot_general(w_conv[9 * depth_tap + 3 * row_tap + col_tap], window, ((...  9.18 us
    all_to_all x1, waiting for transfers between devices, local(): lax.all_to_all(skip, 'space', split_axis=1, concat_axis=2, tiled=True)  9.1 us
    dot_general x27, matrix products, conv_forward(): jnp.dot(w_conv[9 * depth_tap + 3 * row_tap + col_tap], window, preferred_...  8.9 us
    all_to_all x1, starting transfers between devices, local(): lax.all_to_all(skip_part, 'space', split_axis=2, concat_axis=1, tiled=True)  8.65 us
  transfers between devices with their start and end apart: 7, of which 5 were waited for; matrix products, arithmetic and copies ran while one was open for 4% of the time, Pallas kernels for 0%

commit v1 on v0

--- a/solution.py
+++ b/solution.py
@@ -1,8 +1,11 @@
+import functools
 import math
 
 import jax
 import jax.numpy as jnp
 from jax import lax
+from jax.experimental import pallas as pl
+from jax.experimental.pallas import tpu as pltpu
 from jax.sharding import PartitionSpec as P
 
 W = 128
@@ -155,7 +158,372 @@
     return (activation, grad_input, grad_skip, summed_up, summed_conv)
 
 
+H = 8
+ROW = (H + 2) * W
+PLANE = H * W
+PART = 144
+F32 = jnp.float32
+BF16 = jnp.bfloat16
+
+
+def remote(src, dst, send, recv, peer):
+    return pltpu.make_async_remote_copy(
+        src_ref=src,
+        dst_ref=dst,
+        send_sem=send,
+        recv_sem=recv,
+        device_id={"space": peer},
+        device_id_type=pl.DeviceIdType.MESH,
+    )
+
+
+def mm(a, b):
+    return jnp.dot(a, b, preferred_element_type=F32)
+
+
+def mm_nt(a, b):
+    return lax.dot_general(a, b, (((1,), (1,)), ((), ())), preferred_element_type=F32)
+
+
+def mm_tn(a, b):
+    return lax.dot_general(a, b, (((0,), (0,)), ((), ())), preferred_element_type=F32)
+
+
+def fused_kernel(
+    n, scale,
+    coarse, skip, cot, w_up, w_conv,
+    act_out, gin_out, gskip_out, gup_out, gconv_out,
+    w_f, w_u, c_halo, s_got, s_planes, x_buf, g_planes, g_buf, t_send, t_got,
+    part, pair, total, got, full, send, recv,
+):
+    me = lax.axis_index("space")
+    chips = n // 2
+    core = lax.rem(me, 2)
+    chip = lax.div(me, 2)
+    partner = me + 1 - 2 * core
+    half = chips * PART
+    mine = pl.multiple_of(core * half, 16)
+    other = pl.multiple_of((1 - core) * half, 16)
+    lane = lax.broadcasted_iota(jnp.int32, (64, W), 1)
+    low = lane < 64
+
+    c_halo[...] = jnp.zeros_like(c_halo)
+    s_planes[...] = jnp.zeros_like(s_planes)
+    g_planes[...] = jnp.zeros_like(g_planes)
+
+    barrier = pltpu.get_barrier_semaphore()
+
+    @pl.loop(1, n)
+    def _(k):
+        pl.semaphore_signal(
+            barrier, inc=1, device_id={"space": lax.rem(me + k, n)},
+            device_id_type=pl.DeviceIdType.MESH,
+        )
+
+    pl.semaphore_wait(barrier, n - 1)
+
+    def skip_copy(k):
+        peer = lax.rem(me + k, n)
+        return remote(skip.at[peer], s_got.at[me], send.at[0, k], recv.at[0, k], peer)
+
+    @pl.loop(1, n)
+    def _(k):
+        skip_copy(k).start()
+
+    def halo(src_up, src_down, dst_prev, dst_next, index):
+        up = remote(src_up, dst_prev, send.at[1, index], recv.at[1, index], me + 1)
+        down = remote(src_down, dst_next, send.at[1, index + 1], recv.at[1, index + 1], me - 1)
+
+        def start():
+            pl.when(me < n - 1)(up.start)
+            pl.when(me > 0)(down.start)
+
+        def wait():
+            pl.when(me < n - 1)(up.wait_send)
+            pl.when(me > 0)(down.wait_send)
+            pl.when(me > 0)(up.wait_recv)
+            pl.when(me < n - 1)(down.wait_recv)
+
+        return start, wait
+
+    c_start, c_wait = halo(coarse, coarse, c_halo.at[0], c_halo.at[1], 0)
+    c_start()
+
+    x_buf[...] = jnp.zeros_like(x_buf)
+    g_buf[...] = jnp.zeros_like(g_buf)
+    for a in range(3):
+        for b in range(3):
+            for c in range(3):
+                ab = 3 * a + b
+                w_f[64 * c : 64 * c + 64, 128 * ab : 128 * ab + 128] = w_conv[9 * a + 3 * b + c]
+    for ij in range(4):
+        for k in range(2):
+            w_u[64 * ij : 64 * ij + 64, 128 * k : 128 * k + 128] = w_up[2 * ij + k]
+
+    source = lax.broadcasted_iota(jnp.int32, (W, W), 0)
+    target = lax.broadcasted_iota(jnp.int32, (W, W), 1)
+
+    def spread(h2, k):
+        return jnp.where(target == 2 * (source - 64 * h2) + k, 1.0, 0.0).astype(BF16)
+
+    spreads = [[jnp.where((source >= 64 * h2) & (source < 64 * h2 + 64), spread(h2, k), 0) for k in range(2)] for h2 in range(2)]
+
+    def expand(value):
+        return jnp.concatenate(
+            [
+                jnp.concatenate(
+                    [mm(value[:, 128 * (h // 2) : 128 * (h // 2) + 128], spreads[h % 2][k]) for h in range(H // 2)],
+                    axis=1,
+                )
+                for k in range(2)
+            ],
+            axis=0,
+        ).astype(BF16)
+
+    def place(value, plane, j):
+        for h in range(H // 2):
+            at = plane * ROW + (2 * h + j + 1) * W
+            x_buf[0:64, at : at + W] = value[:, h * W : (h + 1) * W].astype(BF16)
+
+    c_exp = expand(coarse[...])
+    up = mm(w_u[...], c_exp)
+    for ij in range(4):
+        place(up[64 * ij : 64 * ij + 64], 1 + ij // 2, ij % 2)
+    c_wait()
+    up = mm(w_u[128:256], expand(c_halo[0]))
+    place(up[0:64], 0, 0)
+    place(up[64:128], 0, 1)
+    up = mm(w_u[0:128], expand(c_halo[1]))
+    place(up[0:64], 3, 0)
+    place(up[64:128], 3, 1)
+
+    @pl.loop(1, n)
+    def _(k):
+        skip_copy(k).wait()
+
+    s_got[me] = skip[me]
+    for h in range(H):
+        left = s_got[2 * h].astype(F32)
+        right = s_got[2 * h + 1].astype(F32)
+        first = jnp.where(low, left, pltpu.roll(right, 64, 1)).astype(BF16)
+        second = jnp.where(low, pltpu.roll(left, 64, 1), right).astype(BF16)
+        s_planes[1, :, h * W : (h + 1) * W] = first
+        s_planes[2, :, h * W : (h + 1) * W] = second
+    s_start, s_wait = halo(s_planes.at[2], s_planes.at[1], s_planes.at[0], s_planes.at[3], 2)
+    s_start()
+    for plane in (1, 2):
+        x_buf[64:128, plane * ROW + W : plane * ROW + W + PLANE] = s_planes[plane]
+    s_wait()
+    for plane in (0, 3):
+        x_buf[64:128, plane * ROW + W : plane * ROW + W + PLANE] = s_planes[plane]
+
+    def windows(buf, plane, sign):
+        parts = []
+        for a in range(3):
+            for b in range(3):
+                at = (plane + 1 + sign * (a - 1)) * ROW + W + sign * (b - 1) * W
+                parts.append(buf[:, at : at + PLANE])
+        return jnp.concatenate(parts, axis=0)
+
+    for plane in range(2):
+        y = mm(w_f[...], windows(x_buf, plane, 1))
+        for h in range(H):
+            at = slice(h * W, (h + 1) * W)
+            full_at = slice(plane * PLANE + h * W, plane * PLANE + (h + 1) * W)
+            pre = (
+                y[64:128, at]
+                + jnp.where(lane > 0, pltpu.roll(y[0:64, at], 1, 1), 0.0)
+                + jnp.where(lane < W - 1, pltpu.roll(y[128:192, at], W - 1, 1), 0.0)
+            )
+            gate = 1.0 / (1.0 + jnp.exp(-pre))
+            act_out[:, full_at] = (pre * gate).astype(BF16)
+            grad = cot[:, full_at].astype(F32) * gate * (1.0 + pre * (1.0 - gate))
+            g_planes[plane + 1, :, at] = grad.astype(BF16)
+
+    g_start, g_wait = halo(g_planes.at[2], g_planes.at[1], g_planes.at[0], g_planes.at[3], 4)
+    g_start()
+
+    def fill(plane):
+        for h in range(H):
+            value = g_planes[plane, :, h * W : (h + 1) * W]
+            wide = value.astype(F32)
+            at = plane * ROW + (h + 1) * W
+            g_buf[64:128, at : at + W] = value
+            g_buf[0:64, at : at + W] = jnp.where(lane < W - 1, pltpu.roll(wide, W - 1, 1), 0.0).astype(BF16)
+            g_buf[128:192, at : at + W] = jnp.where(lane > 0, pltpu.roll(wide, 1, 1), 0.0).astype(BF16)
+
+    fill(1)
+    fill(2)
+
+    d_conv = None
+    for plane in range(2):
+        at = (plane + 1) * ROW + W
+        term = mm_nt(g_buf[:, at : at + PLANE], windows(x_buf, plane, 1))
+        d_conv = term if d_conv is None else d_conv + term
+    for a in range(3):
+        for b in range(3):
+            for c in range(3):
+                ab = 3 * a + b
+                row = 64 * (9 * a + 3 * b + c)
+                part[row : row + 64, :] = d_conv[64 * c : 64 * c + 64, 128 * ab : 128 * ab + 128].astype(BF16)
+
+    g_wait()
+    fill(0)
+    fill(3)
+    w_b = w_conv[...].reshape(27 * 64, 128)
+    joined = [mm_tn(w_b, windows(g_buf, plane, -1)) for plane in range(2)]
+    for h in range(H):
+        at = slice(h * W, (h + 1) * W)
+        first, second = joined[0][64:128, at], joined[1][64:128, at]
+        t_send[2 * h] = jnp.where(low, first, pltpu.roll(second, 64, 1)).astype(BF16)
+        t_send[2 * h + 1] = jnp.where(low, pltpu.roll(first, 64, 1), second).astype(BF16)
+
+    def grad_copy(k):
+        peer = lax.rem(me + k, n)
+        return remote(t_send.at[peer], t_got.at[me], send.at[2, k], recv.at[2, k], peer)
+
+    @pl.loop(1, n)
+    def _(k):
+        grad_copy(k).start()
+
+    g_up = jnp.concatenate(
+        [
+            jnp.concatenate([joined[ij // 2][0:64, (2 * h + ij % 2) * W : (2 * h + ij % 2 + 1) * W] for h in range(H // 2)], axis=1)
+            for ij in range(4)
+        ],
+        axis=0,
+    ).astype(BF16)
+    d_up = mm_nt(g_up, c_exp)
+    for ij in range(4):
+        for k in range(2):
+            row = 64 * (27 + 2 * ij + k)
+            part[row : row + 64, :] = d_up[64 * ij : 64 * ij + 64, 128 * k : 128 * k + 128].astype(BF16)
+    part[35 * 64 :, :] = jnp.zeros((n * PART - 35 * 64, 128), BF16)
+
+    swap = remote(part.at[pl.ds(other, half)], pair, send.at[5, 0], recv.at[5, 0], partner)
+    swap.start()
+
+    squeeze = jnp.where(source == 2 * lax.rem(target, 64) + lax.div(target, 64), 1.0, 0.0).astype(BF16)
+    wide_low = lax.broadcasted_iota(jnp.int32, (128, W), 1) < 64
+    packed = [mm(g_up[:, h * W : (h + 1) * W], squeeze).astype(BF16) for h in range(H // 2)]
+    both = mm_tn(w_u[...], jnp.concatenate(packed, axis=1))
+    for h in range(0, H // 2, 2):
+        z0 = both[0:128, h * W : (h + 1) * W] + pltpu.roll(both[128:256, h * W : (h + 1) * W], 64, 1)
+        z1 = pltpu.roll(both[0:128, (h + 1) * W : (h + 2) * W], 64, 1) + both[128:256, (h + 1) * W : (h + 2) * W]
+        gin_out[:, h * 64 : h * 64 + 128] = jnp.where(wide_low, z0, z1).astype(BF16)
+
+    swap.wait()
+    total[...] = (part[pl.ds(mine, half), :].astype(F32) + pair[...].astype(F32)).astype(BF16)
+
+    def chunk(index):
+        return pl.ds(pl.multiple_of(index * PART, 16), PART)
+
+    def reduce_copy(k):
+        peer = lax.rem(chip + k, chips)
+        return remote(total.at[chunk(peer)], got.at[k], send.at[3, k], recv.at[3, k], 2 * peer + core)
+
+    @pl.loop(1, chips)
+    def _(k):
+        reduce_copy(k).start()
+
+    @pl.loop(1, chips)
+    def _(k):
+        reduce_copy(k).wait()
+
+    summed = total[chunk(chip), :].astype(F32)
+    for k in range(1, chips):
+        summed = summed + got[k].astype(F32)
+    own = pl.ds(pl.multiple_of(core * half + chip * PART, 16), PART)
+    full[own, :] = (summed * scale).astype(BF16)
+
+    def gather_copy(k):
+        peer = lax.rem(chip + k, chips)
+        return remote(full.at[own], full.at[own], send.at[4, k], recv.at[4, k], 2 * peer + core)
+
+    @pl.loop(1, chips)
+    def _(k):
+        gather_copy(k).start()
+
+    @pl.loop(1, n)
+    def _(k):
+        grad_copy(k).wait()
+
+    t_got[me] = t_send[me]
+    gskip_out[...] = t_got[...]
+
+    @pl.loop(1, chips)
+    def _(k):
+        gather_copy(k).wait()
+
+    back = remote(full.at[pl.ds(mine, half)], full.at[pl.ds(mine, half)], send.at[5, 1], recv.at[5, 1], partner)
+    back.start()
+    back.wait()
+    for tap in range(27):
+        gconv_out[tap] = full[64 * tap : 64 * tap + 64, :].astype(F32)
+    for tap in range(8):
+        gup_out[tap] = full[64 * (27 + tap) : 64 * (28 + tap), :].astype(F32)
+
+
+def fused_local(coarse_input, skip, cotangent, w_up, w_conv):
+    n = lax.axis_size("space")
+    planes = cotangent.shape[1]
+    cells = cotangent.shape[2]
+    skip_rows = skip.reshape(64, n, 128).transpose(1, 0, 2)
+    scale = 1.0 / math.sqrt(n * planes * cells)
+    shape = jax.ShapeDtypeStruct
+    vmem = pl.BlockSpec(memory_space=pltpu.VMEM)
+    half = n // 2 * PART
+    act, grad_in, grad_skip, d_up, d_conv = pl.pallas_call(
+        functools.partial(fused_kernel, n, scale),
+        out_shape=(
+            shape((64, 2 * PLANE), BF16),
+            shape((128, 256), BF16),
+            shape((n, 64, 128), BF16),
+            shape((8, 64, 128), F32),
+            shape((27, 64, 128), F32),
+        ),
+        in_specs=[vmem] * 5,
+        out_specs=(vmem,) * 5,
+        scratch_shapes=[
+            pltpu.VMEM((192, 1152), BF16),
+            pltpu.VMEM((256, 256), BF16),
+            pltpu.VMEM((2, 128, 256), BF16),
+            pltpu.VMEM((n, 64, 128), BF16),
+            pltpu.VMEM((4, 64, PLANE), BF16),
+            pltpu.VMEM((128, 4 * ROW), BF16),
+            pltpu.VMEM((4, 64, PLANE), BF16),
+            pltpu.VMEM((192, 4 * ROW), BF16),
+            pltpu.VMEM((n, 64, 128), BF16),
+            pltpu.VMEM((n, 64, 128), BF16),
+            pltpu.VMEM((n * PART, 128), BF16),
+            pltpu.VMEM((half, 128), BF16),
+            pltpu.VMEM((half, 128), BF16),
+            pltpu.VMEM((n // 2, PART, 128), BF16),
+            pltpu.VMEM((n * PART, 128), BF16),
+            pltpu.SemaphoreType.DMA((6, n)),
+            pltpu.SemaphoreType.DMA((6, n)),
+        ],
+        compiler_params=pltpu.CompilerParams(
+            collective_id=0, has_side_effects=True, vmem_limit_bytes=50 * 1024 * 1024
+        ),
+    )(
+        coarse_input.reshape(128, 256),
+        skip_rows,
+        cotangent.reshape(64, 2 * PLANE),
+        w_up,
+        w_conv,
+    )
+    return (
+        act.reshape(64, planes, cells),
+        grad_in.reshape(128, 1, 256),
+        grad_skip.transpose(1, 0, 2).reshape(64, planes * n, 64),
+        d_up,
+        d_conv,
+    )
+
+
 def solution(mesh):
+    body = fused_local if mesh.shape["space"] == 2 * H else local
     in_specs = (
         P("groups", "space", None),
         P("groups", None, "space"),
@@ -170,4 +538,4 @@
         P("groups", None, None),
         P("groups", None, None),
     )
-    return jax.shard_map(local, mesh=mesh, in_specs=in_specs, out_specs=out_specs, check_vma=False)
+    return jax.shard_map(body, mesh=mesh, in_specs=in_specs, out_specs=out_specs, check_vma=False)

time: 212 us -> 54.5 us (0.26)
  waiting for transfers between devices: 97.1 us -> 0 us
  Pallas kernels: 0 us -> 46.9 us
  matrix products: 45.7 us -> 0 us
  starting transfers between devices: 26.8 us -> 0 us
  local copies, waits for them, and re-layouts: 23.3 us -> 6.72 us
  between operations: 15.1 us -> 0.71 us
  other arithmetic: 3.59 us -> 0 us
    psum x1 -> x0, waiting for transfers between devices: 75.4 us -> none  [local(): lax.psum((local_up * scale, local_conv * scale), 'space')]
    pallas_call x0 -> x1, Pallas kernels: none -> 46.9 us  [fused_local(): pl.pallas_call(functools.partial(fused_kernel, n, scale), out_shape=(shap...]
    dot_general x84 -> x0, matrix products: 45.7 us -> none  [the longest x27 26.1 us: conv_weight_grad(): lax.dot_general(grad_flat, window, (((1,), (1,)), ((), ())), preferred_el...]
    all_to_all x2 -> x0, waiting for transfers between devices: 18.7 us -> none  [the longest x1 9.63 us: local(): lax.all_to_all(skip_part, 'space', split_axis=2, concat_axis=1, tiled=True)]
    all_to_all x2 -> x0, starting transfers between devices: 16 us -> none  [the longest x1 8.65 us: local(): lax.all_to_all(skip_part, 'space', split_axis=2, concat_axis=1, tiled=True)]
    ppermute x4 -> x0, starting transfers between devices: 10.7 us -> none  [the longest x2 8.16 us: padded_2(): before = lax.ppermute(last, axis, up)]
    slice x7 -> x0, local copies, waits for them, and re-layouts: 7.07 us -> none  [the longest x2 4.41 us: conv_forward(): padded[:, depth_tap:depth_tap + planes, row_tap:row_tap + height, col_tap...]
    unnamed x107 -> x12, local copies, waits for them, and re-layouts: 9.8 us -> 3.18 us
  transfers between devices with their start and end apart: 7 -> 0, of which waited for: 5 -> 0; matrix products, arithmetic and copies ran while one was open for 4% -> 0% of each run, Pallas kernels for 0% -> 0%
where the time goes in v1:
time: 54.5 us; the launch traced here: 54.3 us
  Pallas kernels  46.9 us (86%)
  local copies, waits for them, and re-layouts  6.72 us (12%)
  between operations  0.71 us (1%)
    pallas_call x1, Pallas kernels, fused_local(): pl.pallas_call(functools.partial(fused_kernel, n, scale), out_shape=(shap...  46.9 us
    unnamed x12, local copies, waits for them, and re-layouts  3.18 us
    reshape x2, local copies, waits for them, and re-layouts, fused_local(): skip_rows = skip.reshape(64, n, 128).transpose(1, 0, 2)  1.43 us

profile of v1, /device:TPU:0, one launch (start us, length us, event | category | flops | bytes accessed | tf_op | source)
XLA Modules:
  0.0 54.3 jit_solution(9392226549778388699)
XLA Ops:
  0.6 0.0 copy-start.3
  0.6 1.4 %reshape.29 = bf16[64,16,128]{2,1,0:T(8,128)(2,1)S(1)} reshape(bf16[64,32,64]{2,1,0:T(8,128)(2,1)} %param.6) | data formatting | bytes 524288 | tf_op jit(solution)/shard_map/reshape | solution.py:471
  2.0 0.0 copy-start
  2.0 0.1 copy.14
  2.1 0.0 copy-done.3
  2.1 0.0 copy-start.1
  2.1 0.0 copy-start.2
  2.1 0.1 copy.12
  2.2 0.8 %copy-done = bf16[27,64,128]{2,1,0:T(8,128)(2,1)S(1)} copy-done((bf16[27,64,128]{2,1,0:T(8,128)(2,1)S(1)}, bf16[27,64,128]{2,1,0:T(8,128)(2,1)}, u32[]{:S(2)}) %copy-start) | copy-done | bytes 442392
  3.0 0.0 copy-done.1
  3.1 0.0 copy-done.2
  3.1 46.9 %shard_map.92 = (bf16[64,2048]{1,0:T(8,128)(2,1)S(1)}, bf16[128,256]{1,0:T(8,128)(2,1)S(1)}, bf16[16,64,128]{2,1,0:T(8,128)(2,1)S(1)}, f32[8,64,128]{2,1,0:T(8,128)S(1)}, f32[27,64,128]{2,1,0:T(8,128)S(1)}) custom-call(bf16[128,256]{1,0:T(8,128)(2,1)S(1)} %bitcast.11, bf16[16,64,128]{2,1,0:T(8,128)(2,1)S(1)} %bitcast.8, bf16[64,2048]{1,0:T(8,128)(2,1)S(1)} %bitcast.9, ...), custom_call_target="tpu_custom_call" | custom-call | tf_op jit(solution)/shard_map/pallas_call | solution.py:476
  50.0 0.2 copy.11
  50.1 1.1 %reshape.33 = bf16[64,32,64]{2,1,0:T(8,128)(2,1)} reshape(bf16[64,16,128]{2,1,0:T(8,128)(2,1)S(1)} %copy.11) | data formatting | bytes 524288 | tf_op jit(solution)/shard_map/reshape | solution.py:519
  51.2 0.9 %reshape.31 = bf16[64,2,1024]{2,1,0:T(2,128)(2,1)} reshape(bf16[64,2048]{1,0:T(8,128)(2,1)S(1)} %get-tuple-element.10) | data formatting | bytes 524288 | tf_op jit(solution)/shard_map/reshape | solution.py:517
  52.1 0.6 %copy.18 = bf16[128,1,256]{2,0,1:T(8,128)(2,1)} copy(bf16[128,1,256]{2,0,1:T(8,128)(2,1)S(1)} %bitcast.12) | data formatting | bytes 131072
  52.7 0.7 %copy.19 = f32[8,64,128]{2,1,0:T(8,128)} copy(f32[8,64,128]{2,1,0:T(8,128)S(1)} %get-tuple-element.23) | data formatting | bytes 524288
  53.4 0.9 %copy.20 = f32[27,64,128]{2,1,0:T(8,128)} copy(f32[27,64,128]{2,1,0:T(8,128)S(1)} %get-tuple-element.24) | data formatting | bytes 1769472
Async XLA Ops:
  0.6 1.5 %copy-start.3 = (bf16[64,2,1024]{2,1,0:T(2,128)(2,1)S(1)}, bf16[64,2,1024]{2,1,0:T(2,128)(2,1)}, u32[]{:S(2)}) copy-start(bf16[64,2,1024]{2,1,0:T(2,128)(2,1)} %param.7) | copy-start | bytes 786436
  2.0 1.0 %copy-start = (bf16[27,64,128]{2,1,0:T(8,128)(2,1)S(1)}, bf16[27,64,128]{2,1,0:T(8,128)(2,1)}, u32[]{:S(2)}) copy-start(bf16[27,64,128]{2,1,0:T(8,128)(2,1)} %w_conv.1) | copy-start | bytes 1327108
  2.1 1.0 %copy-start.1 = (bf16[8,64,128]{2,1,0:T(8,128)(2,1)S(1)}, bf16[8,64,128]{2,1,0:T(8,128)(2,1)}, u32[]{:S(2)}) copy-start(bf16[8,64,128]{2,1,0:T(8,128)(2,1)} %w_up.1) | copy-start | bytes 393220
  2.1 0.9 %copy-start.2 = (bf16[128,1,256]{2,0,1:T(8,128)(2,1)S(1)}, bf16[128,1,256]{2,0,1:T(8,128)(2,1)}, u32[]{:S(2)}) copy-start(bf16[128,1,256]{2,0,1:T(8,128)(2,1)} %param.5) | copy-start | bytes 196612

commit v2 on v1

--- a/solution.py
+++ b/solution.py
@@ -161,7 +161,8 @@
 H = 8
 ROW = (H + 2) * W
 PLANE = H * W
-PART = 144
+CONV_PART = 112
+UP_PART = 32
 F32 = jnp.float32
 BF16 = jnp.bfloat16
 
@@ -189,27 +190,95 @@
     return lax.dot_general(a, b, (((0,), (0,)), ((), ())), preferred_element_type=F32)
 
 
+class Reducer:
+    def __init__(self, me, n, scale, size, part, pair, total, got, full, send, recv, sem):
+        self.chips, self.core, self.chip = n // 2, lax.rem(me, 2), lax.div(me, 2)
+        self.scale, self.size, self.half = scale, size, n // 2 * size
+        self.part, self.pair, self.total, self.got, self.full = part, pair, total, got, full
+        self.send, self.recv, self.sem = send, recv, sem
+        self.partner = me + 1 - 2 * self.core
+        self.mine = pl.ds(pl.multiple_of(self.core * self.half, 16), self.half)
+        self.other = pl.ds(pl.multiple_of((1 - self.core) * self.half, 16), self.half)
+        self.own = pl.ds(pl.multiple_of(self.core * self.half + self.chip * size, 16), size)
+
+    def chunk(self, index):
+        return pl.ds(pl.multiple_of(index * self.size, 16), self.size)
+
+    def swap(self):
+        s = self.sem
+        return remote(self.part.at[self.other], self.pair, self.send.at[s, 0], self.recv.at[s, 0], self.partner)
+
+    def reduce_copy(self, k):
+        peer, s = lax.rem(self.chip + k, self.chips), self.sem
+        return remote(
+            self.total.at[self.chunk(peer)], self.got.at[k], self.send.at[s, k], self.recv.at[s, k],
+            2 * peer + self.core,
+        )
+
+    def gather_copy(self, k):
+        peer, s = lax.rem(self.chip + k, self.chips), self.sem + 1
+        return remote(
+            self.full.at[self.own], self.full.at[self.own], self.send.at[s, k], self.recv.at[s, k],
+            2 * peer + self.core,
+        )
+
+    def back(self):
+        s = self.sem + 1
+        return remote(
+            self.full.at[self.mine], self.full.at[self.mine], self.send.at[s, 0], self.recv.at[s, 0], self.partner
+        )
+
+    def start_swap(self):
+        self.swap().start()
+
+    def start_reduce(self):
+        self.swap().wait()
+        self.total[...] = (self.part[self.mine, :].astype(F32) + self.pair[...].astype(F32)).astype(BF16)
+
+        @pl.loop(1, self.chips)
+        def _(k):
+            self.reduce_copy(k).start()
+
+    def start_gather(self):
+        @pl.loop(1, self.chips)
+        def _(k):
+            self.reduce_copy(k).wait()
+
+        summed = self.total[self.chunk(self.chip), :].astype(F32)
+        for k in range(1, self.chips):
+            summed = summed + self.got[k].astype(F32)
+        self.full[self.own, :] = (summed * self.scale).astype(BF16)
+
+        @pl.loop(1, self.chips)
+        def _(k):
+            self.gather_copy(k).start()
+
+    def start_back(self):
+        @pl.loop(1, self.chips)
+        def _(k):
+            self.gather_copy(k).wait()
+
+        self.back().start()
+
+    def wait_back(self):
+        self.back().wait()
+
+
 def fused_kernel(
     n, scale,
     coarse, skip, cot, w_up, w_conv,
     act_out, gin_out, gskip_out, gup_out, gconv_out,
-    w_f, w_u, c_halo, s_got, s_planes, x_buf, g_planes, g_buf, t_send, t_got,
-    part, pair, total, got, full, send, recv,
+    w_s, w_u, y_buf, c_halo, s_got, s_planes, x_buf, g_planes, g_buf, t_send, t_got,
+    part, pair, total, got, full, u_part, u_pair, u_total, u_got, u_full, send, recv,
 ):
     me = lax.axis_index("space")
-    chips = n // 2
-    core = lax.rem(me, 2)
-    chip = lax.div(me, 2)
-    partner = me + 1 - 2 * core
-    half = chips * PART
-    mine = pl.multiple_of(core * half, 16)
-    other = pl.multiple_of((1 - core) * half, 16)
     lane = lax.broadcasted_iota(jnp.int32, (64, W), 1)
     low = lane < 64
 
     c_halo[...] = jnp.zeros_like(c_halo)
-    s_planes[...] = jnp.zeros_like(s_planes)
-    g_planes[...] = jnp.zeros_like(g_planes)
+    for plane in (0, 3):
+        s_planes[plane] = jnp.zeros((64, PLANE), BF16)
+        g_planes[plane] = jnp.zeros((64, PLANE), BF16)
 
     barrier = pltpu.get_barrier_semaphore()
 
@@ -252,10 +321,13 @@
     x_buf[...] = jnp.zeros_like(x_buf)
     g_buf[...] = jnp.zeros_like(g_buf)
     for a in range(3):
-        for b in range(3):
-            for c in range(3):
-                ab = 3 * a + b
-                w_f[64 * c : 64 * c + 64, 128 * ab : 128 * ab + 128] = w_conv[9 * a + 3 * b + c]
+        for c in range(3):
+            rows = slice(64 * c, 64 * c + 64)
+            t0, t1, t2 = [w_conv[9 * a + 3 * b + c].astype(F32) for b in range(3)]
+            w_s[a, rows, 0:128] = jnp.where(low, t0, pltpu.roll(t1, 64, 1)).astype(BF16)
+            w_s[a, rows, 128:256] = t2.astype(BF16)
+            w_s[3 + a, rows, 0:128] = jnp.where(low, pltpu.roll(t0, 64, 1), t1).astype(BF16)
+            w_s[3 + a, rows, 128:256] = pltpu.roll(t2, 64, 1).astype(BF16)
     for ij in range(4):
         for k in range(2):
             w_u[64 * ij : 64 * ij + 64, 128 * k : 128 * k + 128] = w_up[2 * ij + k]
@@ -296,6 +368,16 @@
     up = mm(w_u[0:128], expand(c_halo[1]))
     place(up[0:64], 3, 0)
     place(up[64:128], 3, 1)
+
+    def forward(side, plane, a):
+        parts = []
+        for b in range(3):
+            at = (plane + a) * ROW + b * W
+            parts.append(x_buf[64 * side : 64 * side + 64, at : at + PLANE])
+        return mm(w_s[3 * side + a, :, 0:192], jnp.concatenate(parts, axis=0))
+
+    for plane in range(2):
+        y_buf[plane] = forward(0, plane, 0) + forward(0, plane, 1) + forward(0, plane, 2)
 
     @pl.loop(1, n)
     def _(k):
@@ -313,6 +395,8 @@
     s_start()
     for plane in (1, 2):
         x_buf[64:128, plane * ROW + W : plane * ROW + W + PLANE] = s_planes[plane]
+    for plane in range(2):
+        y_buf[plane] = y_buf[plane] + (forward(1, plane, 1) + forward(1, plane, 2 - 2 * plane))
     s_wait()
     for plane in (0, 3):
         x_buf[64:128, plane * ROW + W : plane * ROW + W + PLANE] = s_planes[plane]
@@ -326,7 +410,7 @@
         return jnp.concatenate(parts, axis=0)
 
     for plane in range(2):
-        y = mm(w_f[...], windows(x_buf, plane, 1))
+        y = y_buf[plane] + forward(1, plane, 2 * plane)
         for h in range(H):
             at = slice(h * W, (h + 1) * W)
             full_at = slice(plane * PLANE + h * W, plane * PLANE + (h + 1) * W)
@@ -367,11 +451,18 @@
                 row = 64 * (9 * a + 3 * b + c)
                 part[row : row + 64, :] = d_conv[64 * c : 64 * c + 64, 128 * ab : 128 * ab + 128].astype(BF16)
 
+    part[27 * 64 :, :] = jnp.zeros((n * CONV_PART - 27 * 64, 128), BF16)
+    conv_sum = Reducer(me, n, scale, CONV_PART, part, pair, total, got, full, send, recv, 3)
+    up_sum = Reducer(me, n, scale, UP_PART, u_part, u_pair, u_total, u_got, u_full, send, recv, 5)
+    conv_sum.start_swap()
+
     g_wait()
     fill(0)
     fill(3)
     w_b = w_conv[...].reshape(27 * 64, 128)
-    joined = [mm_tn(w_b, windows(g_buf, plane, -1)) for plane in range(2)]
+    joined = [mm_tn(w_b, windows(g_buf, 0, -1))]
+    conv_sum.start_reduce()
+    joined.append(mm_tn(w_b, windows(g_buf, 1, -1)))
     for h in range(H):
         at = slice(h * W, (h + 1) * W)
         first, second = joined[0][64:128, at], joined[1][64:128, at]
@@ -396,12 +487,9 @@
     d_up = mm_nt(g_up, c_exp)
     for ij in range(4):
         for k in range(2):
-            row = 64 * (27 + 2 * ij + k)
-            part[row : row + 64, :] = d_up[64 * ij : 64 * ij + 64, 128 * k : 128 * k + 128].astype(BF16)
-    part[35 * 64 :, :] = jnp.zeros((n * PART - 35 * 64, 128), BF16)
-
-    swap = remote(part.at[pl.ds(other, half)], pair, send.at[5, 0], recv.at[5, 0], partner)
-    swap.start()
+            row = 64 * (2 * ij + k)
+            u_part[row : row + 64, :] = d_up[64 * ij : 64 * ij + 64, 128 * k : 128 * k + 128].astype(BF16)
+    up_sum.start_swap()
 
     squeeze = jnp.where(source == 2 * lax.rem(target, 64) + lax.div(target, 64), 1.0, 0.0).astype(BF16)
     wide_low = lax.broadcasted_iota(jnp.int32, (128, W), 1) < 64
@@ -412,37 +500,9 @@
         z1 = pltpu.roll(both[0:128, (h + 1) * W : (h + 2) * W], 64, 1) + both[128:256, (h + 1) * W : (h + 2) * W]
         gin_out[:, h * 64 : h * 64 + 128] = jnp.where(wide_low, z0, z1).astype(BF16)
 
-    swap.wait()
-    total[...] = (part[pl.ds(mine, half), :].astype(F32) + pair[...].astype(F32)).astype(BF16)
-
-    def chunk(index):
-        return pl.ds(pl.multiple_of(index * PART, 16), PART)
-
-    def reduce_copy(k):
-        peer = lax.rem(chip + k, chips)
-        return remote(total.at[chunk(peer)], got.at[k], send.at[3, k], recv.at[3, k], 2 * peer + core)
-
-    @pl.loop(1, chips)
-    def _(k):
-        reduce_copy(k).start()
-
-    @pl.loop(1, chips)
-    def _(k):
-        reduce_copy(k).wait()
-
-    summed = total[chunk(chip), :].astype(F32)
-    for k in range(1, chips):
-        summed = summed + got[k].astype(F32)
-    own = pl.ds(pl.multiple_of(core * half + chip * PART, 16), PART)
-    full[own, :] = (summed * scale).astype(BF16)
-
-    def gather_copy(k):
-        peer = lax.rem(chip + k, chips)
-        return remote(full.at[own], full.at[own], send.at[4, k], recv.at[4, k], 2 * peer + core)
-
-    @pl.loop(1, chips)
-    def _(k):
-        gather_copy(k).start()
+    conv_sum.start_gather()
+    up_sum.start_reduce()
+    up_sum.start_gather()
 
     @pl.loop(1, n)
     def _(k):
@@ -451,17 +511,14 @@
     t_got[me] = t_send[me]
     gskip_out[...] = t_got[...]
 
-    @pl.loop(1, chips)
-    def _(k):
-        gather_copy(k).wait()
-
-    back = remote(full.at[pl.ds(mine, half)], full.at[pl.ds(mine, half)], send.at[5, 1], recv.at[5, 1], partner)
-    back.start()
-    back.wait()
+    conv_sum.start_back()
+    up_sum.start_back()
+    conv_sum.wait_back()
+    up_sum.wait_back()
     for tap in range(27):
         gconv_out[tap] = full[64 * tap : 64 * tap + 64, :].astype(F32)
     for tap in range(8):
-        gup_out[tap] = full[64 * (27 + tap) : 64 * (28 + tap), :].astype(F32)
+        gup_out[tap] = u_full[64 * tap : 64 * tap + 64, :].astype(F32)
 
 
 def fused_local(coarse_input, skip, cotangent, w_up, w_conv):
@@ -472,7 +529,6 @@
     scale = 1.0 / math.sqrt(n * planes * cells)
     shape = jax.ShapeDtypeStruct
     vmem = pl.BlockSpec(memory_space=pltpu.VMEM)
-    half = n // 2 * PART
     act, grad_in, grad_skip, d_up, d_conv = pl.pallas_call(
         functools.partial(fused_kernel, n, scale),
         out_shape=(
@@ -485,8 +541,9 @@
         in_specs=[vmem] * 5,
         out_specs=(vmem,) * 5,
         scratch_shapes=[
-            pltpu.VMEM((192, 1152), BF16),
+            pltpu.VMEM((6, 192, 256), BF16),
             pltpu.VMEM((256, 256), BF16),
+            pltpu.VMEM((2, 192, PLANE), F32),
             pltpu.VMEM((2, 128, 256), BF16),
             pltpu.VMEM((n, 64, 128), BF16),
             pltpu.VMEM((4, 64, PLANE), BF16),
@@ -495,13 +552,18 @@
             pltpu.VMEM((192, 4 * ROW), BF16),
             pltpu.VMEM((n, 64, 128), BF16),
             pltpu.VMEM((n, 64, 128), BF16),
-            pltpu.VMEM((n * PART, 128), BF16),
-            pltpu.VMEM((half, 128), BF16),
-            pltpu.VMEM((half, 128), BF16),
-            pltpu.VMEM((n // 2, PART, 128), BF16),
-            pltpu.VMEM((n * PART, 128), BF16),
-            pltpu.SemaphoreType.DMA((6, n)),
-            pltpu.SemaphoreType.DMA((6, n)),
+            pltpu.VMEM((n * CONV_PART, 128), BF16),
+            pltpu.VMEM((n // 2 * CONV_PART, 128), BF16),
+            pltpu.VMEM((n // 2 * CONV_PART, 128), BF16),
+            pltpu.VMEM((n // 2, CONV_PART, 128), BF16),
+            pltpu.VMEM((n * CONV_PART, 128), BF16),
+            pltpu.VMEM((n * UP_PART, 128), BF16),
+            pltpu.VMEM((n // 2 * UP_PART, 128), BF16),
+            pltpu.VMEM((n // 2 * UP_PART, 128), BF16),
+            pltpu.VMEM((n // 2, UP_PART, 128), BF16),
+            pltpu.VMEM((n * UP_PART, 128), BF16),
+            pltpu.SemaphoreType.DMA((7, n)),
+            pltpu.SemaphoreType.DMA((7, n)),
         ],
         compiler_params=pltpu.CompilerParams(
             collective_id=0, has_side_effects=True, vmem_limit_bytes=50 * 1024 * 1024

time: 54.5 us -> 57.2 us (1.050)
  Pallas kernels: 46.9 us -> 49.6 us
    pallas_call x1, Pallas kernels: 46.9 us -> 49.6 us  [fused_local(): pl.pallas_call(functools.partial(fused_kernel, n, scale), out_shape=(shap...]
where the time goes in v2:
time: 57.2 us; the launch traced here: 57.1 us
  Pallas kernels  49.6 us (87%)
  local copies, waits for them, and re-layouts  6.72 us (12%)
  between operations  0.71 us (1%)
    pallas_call x1, Pallas kernels, fused_local(): pl.pallas_call(functools.partial(fused_kernel, n, scale), out_shape=(shap...  49.6 us
    unnamed x12, local copies, waits for them, and re-layouts  3.18 us
    reshape x2, local copies, waits for them, and re-layouts, fused_local(): skip_rows = skip.reshape(64, n, 128).transpose(1, 0, 2)  1.43 us

profile of v2, /device:TPU:0, one launch (start us, length us, event | category | flops | bytes accessed | tf_op | source)
XLA Modules:
  0.0 57.1 jit_solution(9880420292646111722)
XLA Ops:
  0.6 0.0 copy-start.3
  0.6 1.4 %reshape.29 = bf16[64,16,128]{2,1,0:T(8,128)(2,1)S(1)} reshape(bf16[64,32,64]{2,1,0:T(8,128)(2,1)} %param.6) | data formatting | bytes 524288 | tf_op jit(solution)/shard_map/reshape | solution.py:528
  2.0 0.0 copy-start
  2.0 0.1 copy.14
  2.1 0.0 copy-done.3
  2.1 0.0 copy-start.1
  2.1 0.0 copy-start.2
  2.1 0.1 copy.12
  2.2 0.8 %copy-done = bf16[27,64,128]{2,1,0:T(8,128)(2,1)S(1)} copy-done((bf16[27,64,128]{2,1,0:T(8,128)(2,1)S(1)}, bf16[27,64,128]{2,1,0:T(8,128)(2,1)}, u32[]{:S(2)}) %copy-start) | copy-done | bytes 442392
  3.0 0.0 copy-done.1
  3.1 0.0 copy-done.2
  3.1 49.6 %shard_map.92 = (bf16[64,2048]{1,0:T(8,128)(2,1)S(1)}, bf16[128,256]{1,0:T(8,128)(2,1)S(1)}, bf16[16,64,128]{2,1,0:T(8,128)(2,1)S(1)}, f32[8,64,128]{2,1,0:T(8,128)S(1)}, f32[27,64,128]{2,1,0:T(8,128)S(1)}) custom-call(bf16[128,256]{1,0:T(8,128)(2,1)S(1)} %bitcast.11, bf16[16,64,128]{2,1,0:T(8,128)(2,1)S(1)} %bitcast.8, bf16[64,2048]{1,0:T(8,128)(2,1)S(1)} %bitcast.9, ...), custom_call_target="tpu_custom_call" | custom-call | tf_op jit(solution)/shard_map/pallas_call | solution.py:532
  52.7 0.2 copy.11
  52.9 1.1 %reshape.33 = bf16[64,32,64]{2,1,0:T(8,128)(2,1)} reshape(bf16[64,16,128]{2,1,0:T(8,128)(2,1)S(1)} %copy.11) | data formatting | bytes 524288 | tf_op jit(solution)/shard_map/reshape | solution.py:581
  53.9 0.9 %reshape.31 = bf16[64,2,1024]{2,1,0:T(2,128)(2,1)} reshape(bf16[64,2048]{1,0:T(8,128)(2,1)S(1)} %get-tuple-element.10) | data formatting | bytes 524288 | tf_op jit(solution)/shard_map/reshape | solution.py:579
  54.8 0.6 %copy.18 = bf16[128,1,256]{2,0,1:T(8,128)(2,1)} copy(bf16[128,1,256]{2,0,1:T(8,128)(2,1)S(1)} %bitcast.12) | data formatting | bytes 131072
  55.5 0.7 %copy.19 = f32[8,64,128]{2,1,0:T(8,128)} copy(f32[8,64,128]{2,1,0:T(8,128)S(1)} %get-tuple-element.23) | data formatting | bytes 524288
  56.2 0.9 %copy.20 = f32[27,64,128]{2,1,0:T(8,128)} copy(f32[27,64,128]{2,1,0:T(8,128)S(1)} %get-tuple-element.24) | data formatting | bytes 1769472
Async XLA Ops:
  0.6 1.5 %copy-start.3 = (bf16[64,2,1024]{2,1,0:T(2,128)(2,1)S(1)}, bf16[64,2,1024]{2,1,0:T(2,128)(2,1)}, u32[]{:S(2)}) copy-start(bf16[64,2,1024]{2,1,0:T(2,128)(2,1)} %param.7) | copy-start | bytes 786436
  2.0 1.0 %copy-start = (bf16[27,64,128]{2,1,0:T(8,128)(2,1)S(1)}, bf16[27,64,128]{2,1,0:T(8,128)(2,1)}, u32[]{:S(2)}) copy-start(bf16[27,64,128]{2,1,0:T(8,128)(2,1)} %w_conv.1) | copy-start | bytes 1327108
  2.1 1.0 %copy-start.1 = (bf16[8,64,128]{2,1,0:T(8,128)(2,1)S(1)}, bf16[8,64,128]{2,1,0:T(8,128)(2,1)}, u32[]{:S(2)}) copy-start(bf16[8,64,128]{2,1,0:T(8,128)(2,1)} %w_up.1) | copy-start | bytes 393220
  2.1 0.9 %copy-start.2 = (bf16[128,1,256]{2,0,1:T(8,128)(2,1)S(1)}, bf16[128,1,256]{2,0,1:T(8,128)(2,1)}, u32[]{:S(2)}) copy-start(bf16[128,1,256]{2,0,1:T(8,128)(2,1)} %param.5) | copy-start | bytes 196612
